TPU v7x, 128 devices: a whole 4x4x4 slice. The times are simulated.
128 devices in a mesh: dp: 8 (over x, core), mp: 16 (over y, z).
Axes of the slice: x: 4, y: 4, z: 4, core: 2. Of those that a mesh axis runs over, the one named last changes fastest.
Arguments:
- features: bfloat16 [131072, 1024], P('dp', 'mp'), may hold values from -6 to 6
- weights1: bfloat16 [1024, 1024], P('mp'), may hold values from -0.1875 to 0.1875
- bias1: float32 [512], replicated, may hold values from -3 to 3
- weights2: bfloat16 [512, 1024], replicated, may hold values from -0.25 to 0.25
- bias2: float32 [512], replicated, may hold values from -3 to 3
- send_rows: int32 [128, 128, 8], P(('dp', 'mp')), may hold values from 0 to 1023
- tile_dst: int32 [128, 128], P(('dp', 'mp')), may hold values from 0 to 7
- tile_src: int32 [128, 128], P(('dp', 'mp')), may hold values from 0 to 15
- tile_count: int32 [128], P(('dp', 'mp')), may hold values from 32 to 128, as said below
- tile_vals: bfloat16 [128, 128, 128, 128], P(('dp', 'mp')), may hold values from 0 to 0.001953125
Outputs:
- embedded: bfloat16 [131072, 512], P(('dp', 'mp'))
Inputs may be any that keep to these rules, and one draw needn't show every extreme that they name: `tile_count`: each partition's slots name distinct pairs of row tile and source tile; one partition has all 128 slots live.
All inputs are finite; a program needn't handle non-finite values.
Results may differ from a plain program's by a relative error of at most 0.004.
Values may be sent and summed in bfloat16 or wider, within the bound.
A program may use at most 192 MiB of HBM per device.

v0:
```python
import jax
import jax.numpy as jnp
from jax import lax
from jax.sharding import PartitionSpec as P

ND = 1024


def aggregate(vals, dst, src, count, source):
    tile = vals.shape[1]
    dst_tiles = ND // tile
    src_tiles = source.shape[0] // tile
    live = (jnp.arange(vals.shape[0], dtype=jnp.int32) < count).astype(jnp.float32)
    dense = jnp.zeros((dst_tiles, src_tiles, tile, tile), jnp.float32)
    dense = dense.at[dst, src].add(vals.astype(jnp.float32) * live[:, None, None])
    dense = (
        dense.transpose(0, 2, 1, 3).reshape(dst_tiles * tile, src_tiles * tile).astype(jnp.bfloat16)
    )
    return jnp.dot(dense, source, preferred_element_type=jnp.float32)


def route_halo(outgoing):
    return lax.all_to_all(outgoing, ("dp", "mp"), split_axis=0, concat_axis=0, tiled=True)


def sage_layer(proj, bias, send_rows, tile_dst, tile_src, tile_count, tile_vals):
    width = bias.shape[0]
    self_part = proj[:, :width]
    neigh = proj[:, width:].astype(jnp.bfloat16)
    outgoing = neigh[send_rows[0]]
    arrived = route_halo(outgoing)
    source = jnp.concatenate([neigh, arrived.reshape(-1, width)], axis=0)
    summed = aggregate(tile_vals[0], tile_dst[0], tile_src[0], tile_count[0], source)
    return self_part + summed + bias


def shards(
    features, weights1, bias1, weights2, bias2, send_rows, tile_dst, tile_src, tile_count, tile_vals
):
    proj1 = lax.psum_scatter(
        jnp.dot(features, weights1, preferred_element_type=jnp.float32),
        "mp",
        scatter_dimension=0,
        tiled=True,
    )
    hidden1 = jax.nn.relu(
        sage_layer(proj1, bias1, send_rows, tile_dst, tile_src, tile_count, tile_vals)
    ).astype(jnp.bfloat16)
    proj2 = jnp.dot(hidden1, weights2, preferred_element_type=jnp.float32)
    return sage_layer(proj2, bias2, send_rows, tile_dst, tile_src, tile_count, tile_vals).astype(
        jnp.bfloat16
    )


def solution(mesh):
    return jax.shard_map(
        shards,
        mesh=mesh,
        in_specs=(
            P("dp", "mp"),
            P("mp", None),
            P(),
            P(),
            P(),
            P(("dp", "mp"), None, None),
            P(("dp", "mp"), None),
            P(("dp", "mp"), None),
            P(("dp", "mp")),
            P(("dp", "mp"), None, None, None),
        ),
        out_specs=P(("dp", "mp"), None),
        check_vma=False,
    )
```

profile of v0, /device:TPU:1, one launch (start us, length us, event | category | flops | bytes accessed | tf_op | source)
XLA Modules:
  0.0 519.3 jit_solution(16847771413524541112)
XLA Ops:
  6.5 0.0 copy-start
  6.5 0.0 reduce-scatter.2.cloned.1.call-start
  6.5 1.6 copy-done
  8.1 24.9 %fusion.38 = f32[16384,1024]{1,0:T(8,128)} fusion(bf16[16384,64]{0,1:T(8,128)(2,1)S(1)} %copy-done, bf16[64,1024]{1,0:T(8,128)(2,1)} %param.11), kind=kOutput, calls=%fused_computation.42 | convolution fusion | flops 2147483648 | bytes 69337088 | tf_op jit(solution)/shard_map/dot_general | solution.py:41
  33.0 0.0 copy-start.1
  33.0 0.0 copy-start.4
  33.0 0.0 copy-start.5
  33.0 0.0 reduce-scatter.2.cloned.1.call-update
  33.0 0.7 copy-done.1
  33.7 0.1 copy.13
  33.8 0.1 reshape.107
  34.6 0.0 copy-done.4
  34.6 0.0 copy-done.5
  34.6 365.2 %reduce-scatter.2.cloned.1.call-done = f32[1024,1024]{1,0:T(8,128)} async-done(((f32[16384,1024]{1,0:T(8,128)}), f32[1024,1024]{1,0:T(8,128)}) %reduce-scatter.2.cloned.1.call-update) | async-done | bytes 4194320 | tf_op jit(solution)/shard_map/reduce_scatter | solution.py:40
  399.8 1.7 slice.45
  401.6 5.1 gather_fusion
  406.6 8.3 %all-to-all-start = ((bf16[128,8,512]{2,1,0:T(8,128)(2,1)}), bf16[128,8,512]{2,1,0:T(8,128)(2,1)}, u32[]{:S(2)}, u32[]{:S(2)}) async-start(bf16[128,8,512]{2,1,0:T(8,128)(2,1)} %bitcast.41), calls=%async_computation.1 | async-start | bytes 2097152 | tf_op jit(solution)/shard_map/all_to_all | solution.py:23
  414.9 6.0 %convert_multiply_fusion = f32[128,128,128]{2,1,0:T(8,128)} fusion(bf16[1,128,128,128]{3,2,1,0:T(8,128)(2,1)} %param.19, f32[128]{0:T(128)S(1)} %compare_convert_fusion), kind=kLoop, calls=%fused_computation.3 | loop fusion | flops 4194304 | bytes 12583424 | tf_op jit(solution)/shard_map/mul | solution.py:15
  420.9 4.3 broadcast.66
  425.2 27.5 %scatter_fusion = f32[8,16,128,128]{3,2,1,0:T(8,128)} fusion(f32[8,16,128,128]{3,2,1,0:T(8,128)} %broadcast.66, s32[128]{0:T(128)S(1)} %fusion.33, f32[128,128,128]{2,1,0:T(8,128)} %convert_multiply_fusion), kind=kCustom, calls=%fused_computation.2 | custom fusion | flops 2097152 | bytes 25166848 | tf_op jit(solution)/shard_map/scatter-add | solution.py:15
  452.7 4.4 convert_bitcast_fusion
  457.1 0.0 copy-start.2
  457.1 4.8 copy.12
  461.9 0.0 all-to-all-done
  461.9 0.0 copy-done.2
  461.9 8.8 %fusion.27 = f32[1024,1024]{1,0:T(8,128)} fusion(bf16[512,1024]{1,0:T(8,128)(2,1)} %param.13, f32[1024,1024]{1,0:T(8,128)} %reduce-scatter.2.cloned.1.call-done, bf16[1024,512]{1,0:T(8,128)(2,1)} %bitcast.8, bf16[1024,512]{1,0:T(8,128)(2,1)S(1)} %slice.45, bf16[128,8,16,128]{3,2,1,0:T(8,128)(2,1)} %bitcast.43, f32[512]{0:T(512)S(1)} %copy-done.2), kind=kOutput, calls=%fused_computation.26 | convolution fusion | flops 3227516928 | bytes 13633536 | tf_op jit(solution)/shard_map/dot_general | solution.py:49
  470.7 1.7 slice.44
  472.4 0.0 copy-start.3
  472.4 5.1 gather_fusion.1
  477.5 28.7 %all_to_all.10 = bf16[128,8,512]{2,1,0:T(8,128)(2,1)S(1)} all-to-all(bf16[128,8,512]{2,1,0:T(8,128)(2,1)} %bitcast.42), channel_id=1, replica_groups=mesh['dp'=8,'mp'=16] {'dp','mp'}, dimensions={0} | all-to-all | bytes 2097152 | tf_op jit(solution)/shard_map/all_to_all | solution.py:23
  506.2 0.0 copy-done.3
  506.2 6.2 %fusion.7 = bf16[1024,512]{1,0:T(8,128)(2,1)} fusion(f32[1024,1024]{1,0:T(8,128)} %fusion.27, bf16[1024,512]{1,0:T(8,128)(2,1)S(1)} %bitcast.45, bf16[1024,512]{1,0:T(8,128)(2,1)S(1)} %slice.44, bf16[128,8,16,128]{3,2,1,0:T(8,128)(2,1)} %bitcast.44, f32[512]{0:T(512)S(1)} %copy-done.3), kind=kOutput, calls=%fused_computation.14 | convolution fusion | flops 2153250816 | bytes 9439232 | tf_op jit(solution)/shard_map/dot_general | solution.py:19
  (4 shorter events, 0.0 us)
Async XLA Ops:
  6.5 1.6 copy-start
  6.5 393.3 %reduce-scatter.2.cloned.1.call-start = ((), (), s32[]{:S(2)}) async-start(), calls=%async_computation.3 | async-start | bytes 71303168 | tf_op jit(solution)/shard_map/reduce_scatter | solution.py:40
  33.0 0.7 copy-start.1
  33.0 1.6 copy-start.4
  33.0 1.6 copy-start.5
  406.6 55.2 %all-to-all-start = ((bf16[128,8,512]{2,1,0:T(8,128)(2,1)}), bf16[128,8,512]{2,1,0:T(8,128)(2,1)}, u32[]{:S(2)}, u32[]{:S(2)}) async-start(bf16[128,8,512]{2,1,0:T(8,128)(2,1)} %bitcast.41), calls=%async_computation.1 | async-start | bytes 2097152 | tf_op jit(solution)/shard_map/all_to_all | solution.py:23
  457.1 4.8 copy-start.2
  472.4 33.8 %copy-start.3 = (f32[512]{0:T(512)S(1)}, f32[512]{0:T(512)}, u32[]{:S(2)}) copy-start(f32[512]{0:T(512)} %param.14) | copy-start | bytes 6148
Sparse Core Ops, SparseCore 0:
  33.2 366.6 reduce-scatter.1
where the time goes:
time: 520 us; the launch traced here: 519 us
  waiting for transfers between devices  365 us (70%)
  matrix products  39.9 us (8%)
  other arithmetic  37.9 us (7%)
  blocking collectives  28.7 us (6%)
  local copies, waits for them, and re-layouts  25.1 us (5%)
  between operations  14.1 us (3%)
  starting transfers between devices  8.26 us (2%)
    reduce_scatter x1, waiting for transfers between devices, shards(): lax.psum_scatter(jnp.dot(features, weights1, preferred_element_type=jnp.f...  365 us
    all_to_all x1, blocking collectives, route_halo(): lax.all_to_all(outgoing, ('dp', 'mp'), split_axis=0, concat_axis=0, tiled...  28.7 us
    scatter-add x1, other arithmetic, aggregate(): dense.at[dst, src].add(vals.astype(jnp.float32) * live[:, None, None])  27.5 us
    dot_general x1, matrix products, shards(): jnp.dot(features, weights1, preferred_element_type=jnp.float32)  24.9 us
  transfers between devices with their start and end apart: 2, of which 1 were waited for; matrix products, arithmetic and copies ran while one was open for 9% of the time, Pallas kernels for 0%

commit v1 on v0

v1 whole, which is shorter than its diff:
```python
import jax
import jax.numpy as jnp
from jax import lax
from jax.sharding import PartitionSpec as P

ND = 1024


def dense_adjacency(vals, dst, src, count):
    pos = dst * 16 + src
    slot = jnp.arange(128, dtype=jnp.int32)
    hit = (pos[None, :] == slot[:, None]) & (slot[None, :] < count)
    inv = jnp.sum(jnp.where(hit, slot[None, :], 0), axis=1)
    live = jnp.any(hit, axis=1)
    tiles = jnp.where(live[:, None, None], vals[inv], 0)
    return tiles.reshape(8, 16, 128, 128).transpose(0, 2, 1, 3).reshape(ND, 2048)


def shards(
    features, weights1, bias1, weights2, bias2, send_rows, tile_dst, tile_src, tile_count, tile_vals
):
    dense = dense_adjacency(tile_vals[0], tile_dst[0], tile_src[0], tile_count[0])
    feats = lax.all_to_all(features.reshape(16, ND, 64), "mp", split_axis=0, concat_axis=0, tiled=True)
    feats = feats.transpose(1, 0, 2).reshape(ND, 1024)
    w1 = lax.all_gather(weights1, "mp", axis=0, tiled=True)
    rows = send_rows[0].reshape(-1)

    def layer(proj, bias):
        neigh = proj[:, 512:].astype(jnp.bfloat16)
        outgoing = neigh[rows].reshape(128, 8, 512)
        arrived = lax.all_to_all(outgoing, ("dp", "mp"), split_axis=0, concat_axis=0, tiled=True)
        source = jnp.concatenate([neigh, arrived.reshape(-1, 512)], axis=0)
        return proj[:, :512] + jnp.dot(dense, source, preferred_element_type=jnp.float32) + bias

    proj1 = jnp.dot(feats, w1, preferred_element_type=jnp.float32)
    hidden1 = jax.nn.relu(layer(proj1, bias1)).astype(jnp.bfloat16)
    proj2 = jnp.dot(hidden1, weights2, preferred_element_type=jnp.float32)
    return layer(proj2, bias2).astype(jnp.bfloat16)


def solution(mesh):
    return jax.shard_map(
        shards,
        mesh=mesh,
        in_specs=(
            P("dp", "mp"),
            P("mp", None),
            P(),
            P(),
            P(),
            P(("dp", "mp"), None, None),
            P(("dp", "mp"), None),
            P(("dp", "mp"), None),
            P(("dp", "mp")),
            P(("dp", "mp"), None, None, None),
        ),
        out_specs=P(("dp", "mp"), None),
        check_vma=False,
    )
```

time: 520 us -> 161 us (0.31)
  waiting for transfers between devices: 365 us -> 59.4 us
  other arithmetic: 37.9 us -> 6.88 us
  matrix products: 39.9 us -> 18.5 us
  starting transfers between devices: 8.26 us -> 17.2 us
  blocking collectives: 28.7 us -> 23.1 us
    reduce_scatter x1 -> x0, waiting for transfers between devices: 365 us -> none  [shards(): lax.psum_scatter(jnp.dot(features, weights1, preferred_element_type=jnp.f...]
    all_to_all x1 -> x2, waiting for transfers between devices: 0.01 us -> 35.8 us  [the longest x1 29.1 us: shards(): lax.all_to_all(features.reshape(16, ND, 64), 'mp', split_axis=0, concat_a...]
    scatter-add x1 -> x0, other arithmetic: 27.5 us -> none  [aggregate(): dense.at[dst, src].add(vals.astype(jnp.float32) * live[:, None, None])]
    all_gather x0 -> x1, waiting for transfers between devices: none -> 22.9 us  [shards(): w1 = lax.all_gather(weights1, 'mp', axis=0, tiled=True)]
    dot_general x2, matrix products: 31.1 us -> 10.2 us  [the longest x1 6.18 us: layer(): jnp.dot(dense, source, preferred_element_type=jnp.float32)]
    all_to_all x1 -> x2, starting transfers between devices: 8.26 us -> 17.2 us  [the longest x1 8.6 us: shards(): lax.all_to_all(features.reshape(16, ND, 64), 'mp', split_axis=0, concat_a...]
    select_n x1 -> x3, other arithmetic: 0.01 us -> 6.63 us  [the longest x2 6.62 us: dense_adjacency(): tiles = jnp.where(live[:, None, None], vals[inv], 0)]
    mul x1 -> x0, other arithmetic: 6.01 us -> none  [aggregate(): vals.astype(jnp.float32) * live[:, None, None]]
  transfers between devices with their start and end apart: 2 -> 3, of which waited for: 1 -> 3; matrix products, arithmetic and copies ran while one was open for 9% -> 10% of each run, Pallas kernels for 0% -> 0%
where the time goes in v1:
time: 161 us
  waiting for transfers between devices  59.4 us (37%)
  blocking collectives  23.1 us (14%)
  local copies, waits for them, and re-layouts  21.6 us (13%)
  matrix products  18.5 us (11%)
  starting transfers between devices  17.2 us (11%)
  between operations  14.2 us (9%)
  other arithmetic  6.88 us (4%)
    all_to_all x1, waiting for transfers between devices, shards(): lax.all_to_all(features.reshape(16, ND, 64), 'mp', split_axis=0, concat_a...  29.1 us
    all_to_all x1, blocking collectives, layer(): lax.all_to_all(outgoing, ('dp', 'mp'), split_axis=0, concat_axis=0, tiled...  23.1 us
    all_gather x1, waiting for transfers between devices, shards(): w1 = lax.all_gather(weights1, 'mp', axis=0, tiled=True)  22.9 us
    gather x2, local copies, waits for them, and re-layouts, layer(): outgoing = neigh[rows].reshape(128, 8, 512)  9.05 us
    all_to_all x1, starting transfers between devices, shards(): lax.all_to_all(features.reshape(16, ND, 64), 'mp', split_axis=0, concat_a...  8.6 us
    all_to_all x1, starting transfers between devices, layer(): lax.all_to_all(outgoing, ('dp', 'mp'), split_axis=0, concat_axis=0, tiled...  8.57 us
    dot_general x1, matrix products, shards(): proj2 = jnp.dot(hidden1, weights2, preferred_element_type=jnp.float32)  8.27 us
    all_to_all x1, waiting for transfers between devices, layer(): lax.all_to_all(outgoing, ('dp', 'mp'), split_axis=0, concat_axis=0, tiled...  6.7 us
  transfers between devices with their start and end apart: 3, of which 3 were waited for; matrix products, arithmetic and copies ran while one was open for 10% of the time, Pallas kernels for 0%

profile of v1, /device:TPU:1, one launch (start us, length us, event | category | flops | bytes accessed | tf_op | source)
XLA Modules:
  0.0 160.8 jit_solution(489408609561463816)
XLA Ops:
  6.5 0.0 copy-start
  6.5 0.0 all-gather.2.cloned.1.call-start
  6.5 0.7 all-gather.2.cloned.1.call-update
  7.3 0.0 copy-start.2
  7.3 0.0 copy-start.5
  7.3 0.0 copy-start.6
  7.3 3.2 %copy.40 = bf16[8,16,8,1024]{3,2,0,1:T(8,128)(2,1)} copy(bf16[8,16,8,1024]{3,2,1,0:T(8,128)(2,1)} %bitcast.44) | data formatting | bytes 4194304 | tf_op jit(solution)/shard_map/reshape | solution.py:23
  10.4 8.6 %all-to-all-start = ((bf16[16,1024,64]{1,2,0:T(8,128)(2,1)}), bf16[16,1024,64]{1,2,0:T(8,128)(2,1)S(1)}, u32[]{:S(2)}, u32[]{:S(2)}) async-start(bf16[16,1024,64]{1,2,0:T(8,128)(2,1)} %bitcast.37), calls=%async_computation | async-start | bytes 4194304 | tf_op jit(solution)/shard_map/all_to_all | solution.py:23
  19.7 0.0 copy-done.2
  19.7 0.1 copy.21
  19.8 0.1 reshape_squeeze.3
  19.9 0.0 copy-done.5
  19.9 0.0 copy-done.6
  20.0 29.1 %all-to-all-done = bf16[16,1024,64]{1,2,0:T(8,128)(2,1)S(1)} async-done(((bf16[16,1024,64]{1,2,0:T(8,128)(2,1)}), bf16[16,1024,64]{1,2,0:T(8,128)(2,1)S(1)}, u32[]{:S(2)}, u32[]{:S(2)}) %all-to-all-start) | async-done | bytes 2097184 | tf_op jit(solution)/shard_map/all_to_all | solution.py:23
  49.1 22.9 %all-gather.2.cloned.1.call-done = bf16[1024,1024]{1,0:T(8,128)(2,1)} async-done(((bf16[64,1024]{1,0:T(8,128)(2,1)}), bf16[1024,1024]{1,0:T(8,128)(2,1)}) %all-gather.2.cloned.1.call-update) | async-done | bytes 2097168 | tf_op jit(solution)/shard_map/all_gather | solution.py:25
  72.0 4.0 %fusion.39 = f32[1024,1024]{1,0:T(8,128)S(1)} fusion(bf16[1024,1024]{0,1:T(8,128)(2,1)S(1)} %bitcast.45, bf16[1024,1024]{1,0:T(8,128)(2,1)} %all-gather.2.cloned.1.call-done), kind=kOutput, calls=%fused_computation.43 | convolution fusion | flops 2147483648 | bytes 8388608 | tf_op jit(solution)/shard_map/dot_general | solution.py:35
  76.0 0.0 copy-start.1
  76.0 1.9 %copy-done.1 = f32[1024,1024]{1,0:T(8,128)} copy-done((f32[1024,1024]{1,0:T(8,128)}, f32[1024,1024]{1,0:T(8,128)S(1)}, u32[]{:S(2)}) %copy-start.1) | copy-done | bytes 4194328
  77.9 0.2 slice.45
  78.1 5.1 %gather_fusion.1 = bf16[1024,512]{1,0:T(8,128)(2,1)} fusion(bf16[1024,512]{1,0:T(8,128)(2,1)S(1)} %slice.45, s32[1024]{0:T(1024)S(1)} %broadcast_clamp_fusion), kind=kCustom, calls=%fused_computation.1 | custom fusion | bytes 2101248 | tf_op jit(solution)/shard_map/gather | solution.py:30
  83.2 8.6 %all-to-all-start.1 = ((bf16[128,8,512]{2,1,0:T(8,128)(2,1)}), bf16[128,8,512]{2,1,0:T(8,128)(2,1)S(1)}, u32[]{:S(2)}, u32[]{:S(2)}) async-start(bf16[128,8,512]{2,1,0:T(8,128)(2,1)} %bitcast.10), calls=%async_computation.1 | async-start | bytes 2097152 | tf_op jit(solution)/shard_map/all_to_all | solution.py:31
  91.8 0.1 fusion.33
  91.9 0.1 broadcast_in_dim.36
  92.0 0.1 select_reduce_fusion
  92.1 5.2 %gather_fusion = bf16[128,128,128]{2,1,0:T(8,128)(2,1)} fusion(bf16[128,128,128]{2,1,0:T(8,128)(2,1)} %bitcast.41, s32[1024]{0:T(1024)S(1)} %pad_clamp_fusion), kind=kCustom, calls=%fused_computation | custom fusion | bytes 8389120 | tf_op jit(solution)/shard_map/gather | solution.py:15
  97.4 0.0 copy-start.3
  97.4 6.6 %copy_select_fusion = bf16[8,16,128,128]{3,1,2,0:T(8,128)(2,1)} fusion(bf16[8,16,128,128]{3,2,1,0:T(8,128)(2,1)} %bitcast.39, pred[8,16]{1,0:T(8,128)(4,1)S(1)} %broadcast_in_dim.36), kind=kLoop, calls=%fused_computation.7 | loop fusion | flops 2097152 | bytes 8388736 | tf_op jit(solution)/shard_map/jit(_where)/select_n | solution.py:15
  104.0 6.7 %all-to-all-done.1 = bf16[128,8,512]{2,1,0:T(8,128)(2,1)S(1)} async-done(((bf16[128,8,512]{2,1,0:T(8,128)(2,1)}), bf16[128,8,512]{2,1,0:T(8,128)(2,1)S(1)}, u32[]{:S(2)}, u32[]{:S(2)}) %all-to-all-start.1) | async-done | bytes 1048608 | tf_op jit(solution)/shard_map/all_to_all | solution.py:31
  110.7 0.0 copy-done
  110.7 0.0 copy-done.3
  110.7 8.3 %fusion.27 = f32[1024,1024]{1,0:T(8,128)} fusion(bf16[512,1024]{1,0:T(8,128)(2,1)S(1)} %copy-done, f32[1024,1024]{1,0:T(8,128)} %copy-done.1, bf16[1024,512]{1,0:T(8,128)(2,1)S(1)} %bitcast.46, bf16[1024,512]{1,0:T(8,128)(2,1)S(1)} %slice.45, bf16[128,8,16,128]{3,2,1,0:T(8,128)(2,1)} %bitcast.42, f32[512]{0:T(512)S(1)} %copy-done.3), kind=kOutput, calls=%fused_computation.26 | convolution fusion | flops 3227516928 | bytes 13633536 | tf_op jit(solution)/shard_map/dot_general | solution.py:37
  119.0 1.7 %slice.44 = bf16[1024,512]{1,0:T(8,128)(2,1)S(1)} slice(f32[1024,1024]{1,0:T(8,128)} %fusion.27), slice={[0:1024], [512:1024]} | slice | bytes 2097152 | tf_op jit(solution)/shard_map/slice | solution.py:29
  120.7 0.0 copy-start.4
  120.7 4.0 %gather_fusion.2 = bf16[1024,512]{1,0:T(8,128)(2,1)S(1)} fusion(bf16[1024,512]{1,0:T(8,128)(2,1)S(1)} %slice.44, s32[1024]{0:T(1024)S(1)} %broadcast_clamp_fusion), kind=kCustom, calls=%fused_computation.2 | custom fusion | bytes 2101248 | tf_op jit(solution)/shard_map/gather | solution.py:30
  124.7 23.1 %all_to_all.15 = bf16[128,8,512]{2,1,0:T(8,128)(2,1)S(1)} all-to-all(bf16[128,8,512]{2,1,0:T(8,128)(2,1)S(1)} %bitcast.40), channel_id=1, replica_groups=mesh['dp'=8,'mp'=16] {'dp','mp'}, dimensions={0} | all-to-all | bytes 2097152 | tf_op jit(solution)/shard_map/all_to_all | solution.py:31
  147.8 0.0 copy-done.4
  147.8 6.2 %fusion.7 = bf16[1024,512]{1,0:T(8,128)(2,1)} fusion(f32[1024,1024]{1,0:T(8,128)} %fusion.27, bf16[1024,512]{1,0:T(8,128)(2,1)S(1)} %bitcast.47, bf16[1024,512]{1,0:T(8,128)(2,1)S(1)} %slice.44, bf16[128,8,16,128]{3,2,1,0:T(8,128)(2,1)} %bitcast.43, f32[512]{0:T(512)S(1)} %copy-done.4), kind=kOutput, calls=%fused_computation.14 | convolution fusion | flops 2153250816 | bytes 9439232 | tf_op jit(solution)/shard_map/dot_general | solution.py:33
  (6 shorter events, 0.0 us)
Async XLA Ops:
  6.5 104.2 %copy-start = (bf16[512,1024]{1,0:T(8,128)(2,1)S(1)}, bf16[512,1024]{1,0:T(8,128)(2,1)}, u32[]{:S(2)}) copy-start(bf16[512,1024]{1,0:T(8,128)(2,1)} %param.13) | copy-start | bytes 3145732
  6.5 65.5 %all-gather.2.cloned.1.call-start = ((), (), s32[]{:S(2)}) async-start(), calls=%async_computation.3 | async-start | bytes 2228224 | tf_op jit(solution)/shard_map/all_gather | solution.py:25
  7.3 12.4 %copy-start.2 = (s32[1,128,8]{1,2,0:T(8,128)S(1)}, s32[1,128,8]{1,2,0:T(8,128)}, u32[]{:S(2)}) copy-start(s32[1,128,8]{1,2,0:T(8,128)} %param.15) | copy-start | bytes 12292
  7.3 12.6 %copy-start.5 = (s32[1,128]{1,0:T(1,128)S(1)}, s32[1,128]{1,0:T(1,128)}, u32[]{:S(2)}) copy-start(s32[1,128]{1,0:T(1,128)} %param.17) | copy-start | bytes 1540
  7.3 12.6 %copy-start.6 = (s32[1,128]{1,0:T(1,128)S(1)}, s32[1,128]{1,0:T(1,128)}, u32[]{:S(2)}) copy-start(s32[1,128]{1,0:T(1,128)} %param.16) | copy-start | bytes 1540
  10.4 38.6 %all-to-all-start = ((bf16[16,1024,64]{1,2,0:T(8,128)(2,1)}), bf16[16,1024,64]{1,2,0:T(8,128)(2,1)S(1)}, u32[]{:S(2)}, u32[]{:S(2)}) async-start(bf16[16,1024,64]{1,2,0:T(8,128)(2,1)} %bitcast.37), calls=%async_computation | async-start | bytes 4194304 | tf_op jit(solution)/shard_map/all_to_all | solution.py:23
  76.0 1.9 %copy-start.1 = (f32[1024,1024]{1,0:T(8,128)}, f32[1024,1024]{1,0:T(8,128)S(1)}, u32[]{:S(2)}) copy-start(f32[1024,1024]{1,0:T(8,128)S(1)} %fusion.39) | copy-start | bytes 12582916
  83.2 27.5 %all-to-all-start.1 = ((bf16[128,8,512]{2,1,0:T(8,128)(2,1)}), bf16[128,8,512]{2,1,0:T(8,128)(2,1)S(1)}, u32[]{:S(2)}, u32[]{:S(2)}) async-start(bf16[128,8,512]{2,1,0:T(8,128)(2,1)} %bitcast.10), calls=%async_computation.1 | async-start | bytes 2097152 | tf_op jit(solution)/shard_map/all_to_all | solution.py:31
  97.4 13.3 %copy-start.3 = (f32[512]{0:T(512)S(1)}, f32[512]{0:T(512)}, u32[]{:S(2)}) copy-start(f32[512]{0:T(512)} %param.12) | copy-start | bytes 6148
  120.7 27.1 %copy-start.4 = (f32[512]{0:T(512)S(1)}, f32[512]{0:T(512)}, u32[]{:S(2)}) copy-start(f32[512]{0:T(512)} %param.14) | copy-start | bytes 6148
Sparse Core Ops, SparseCore 0:
  9.5 62.4 all-gather.1

commit v2 on v1

v2 whole, which is shorter than its diff:
```python
import jax
import jax.numpy as jnp
from jax import lax
from jax.experimental import pallas as pl
from jax.experimental.pallas import tpu as pltpu
from jax.sharding import PartitionSpec as P

MESH = pl.DeviceIdType.MESH
ND, F, HID, TILE = 1024, 1024, 512, 128
STEPS = (2, 1, 3, 0)
BF = jnp.bfloat16
F32 = jnp.float32


def dot(a, b):
    return jnp.dot(a, b, preferred_element_type=F32)


def dot_t(a, b):
    return lax.dot_general(a, b, (((0,), (0,)), ((), ())), preferred_element_type=F32)


def kernel(
    feat, w1, bias1, w2, bias2, rows, slot, vals, out,
    xt, w1f, w2v, tiles, adj, pick, acc, neigh, hidden, result,
    outgoing1, outgoing2, halo1, halo2,
    local_sem, x_send, x_recv, w_send, w_recv, h_send, h_recv, o_sem,
):
    dp, mp = lax.axis_index("dp"), lax.axis_index("mp")
    x, c, y, z = dp // 2, dp % 2, mp // 4, mp % 4

    def remote(src, dst, send, recv, to):
        return pltpu.make_async_remote_copy(
            src_ref=src, dst_ref=dst, send_sem=send, recv_sem=recv, device_id=to, device_id_type=MESH
        )

    cb = pl.multiple_of((c * 4 + x) * 128, 128)
    mine = [
        pltpu.make_async_copy(vals, tiles.at[pl.ds(0, 128)], local_sem.at[0]),
        pltpu.make_async_copy(w2, w2v, local_sem.at[1]),
        pltpu.make_async_copy(
            feat.at[:, pl.ds(pl.multiple_of(mp * ND, ND), ND)], xt.at[mp], local_sem.at[2]
        ),
        pltpu.make_async_copy(w1.at[:, pl.ds(cb, 128)], w1f.at[mp, :, pl.ds(cb, 128)], local_sem.at[3]),
    ]
    for copy in mine:
        copy.start()

    barrier = pltpu.get_barrier_semaphore()

    @pl.loop(1, 128)
    def _(i):
        there = lax.rem(dp + i // 16, 8), lax.rem(mp + i % 16, 16)
        pl.semaphore_signal(barrier, inc=1, device_id=there, device_id_type=MESH)

    pl.semaphore_wait(barrier, 127)

    @pl.loop(1, 16)
    def _(i):
        there = lax.rem(y + i // 4, 4) * 4 + lax.rem(z + i % 4, 4)
        remote(
            w1.at[:, pl.ds(cb, 128)], w1f.at[mp, :, pl.ds(cb, 128)], w_send.at[0], w_recv.at[0], (dp, there)
        ).start()

    for g, dy in enumerate(STEPS):
        @pl.loop(1 if dy == 0 else 0, 4)
        def _(i):
            there = lax.rem(y + dy, 4) * 4 + lax.rem(z + i, 4)
            block = pl.ds(pl.multiple_of(there * ND, ND), ND)
            remote(feat.at[:, block], xt.at[mp], x_send, x_recv.at[g], (dp, there)).start()

    table = rows[...]
    lanes = lax.broadcasted_iota(jnp.int32, (16, ND), 1)
    for r in range(0, 128, 2):
        want = jnp.concatenate([table[:, r : r + 1], table[:, r + 1 : r + 2]], axis=0)
        pick[r * 8 : r * 8 + 16, :] = jnp.where(want == lanes, 1.0, 0.0).astype(BF)

    mine[3].wait()
    remote(
        w1f.at[pl.ds(0, 15), :, pl.ds(0, 128)], w1f.at[pl.ds(0, 15), :, pl.ds(0, 128)],
        w_send.at[0], w_recv.at[0], (dp, mp),
    ).wait_recv()
    for dx in (1, 2, 3):
        part = w1f.at[:, :, pl.ds(cb, 128)]
        remote(part, part, w_send.at[1], w_recv.at[1], (lax.rem(x + dx, 4) * 2 + c, mp)).start()

    tiles[128] = jnp.zeros((TILE, TILE), BF)
    mine[0].wait()

    @pl.loop(0, 8)
    def _(d):
        at = pl.ds(pl.multiple_of(d * TILE, TILE), TILE)
        for s in range(16):
            adj[at, s * TILE : (s + 1) * TILE] = tiles[slot[d * 16 + s]]

    others = w1f.at[:, :, pl.ds(0, 384)]
    remote(others, others, w_send.at[1], w_recv.at[1], (dp, mp)).wait_recv()
    half = w1f.at[:, :, pl.ds(pl.multiple_of(c * 512, 512), 512)]
    remote(half, half, w_send.at[2], w_recv.at[2], (x * 2 + 1 - c, mp)).start()
    remote(half, half, w_send.at[2], w_recv.at[2], (dp, mp)).wait_recv()
    mine[2].wait()
    mine[1].wait()

    for g, dy in enumerate(STEPS):
        count = 3 if dy == 0 else 4
        part = xt.at[pl.ds(0, count)]
        remote(part, part, x_send, x_recv.at[g], (dp, mp)).wait_recv()
        src = pl.ds(lax.rem(y + 4 - dy, 4) * 4, 4)
        last = g == 3

        def project(col, m):
            at = pl.ds(pl.multiple_of(m * 256, 256), 256)
            got = dot_t(
                xt[src, :, at].reshape(256, 256), w1f[src, :, col : col + 512].reshape(256, 512)
            )
            if g > 0:
                got = got + acc[at, col : col + 512]
            return at, got

        @pl.loop(0, 4)
        def _(m):
            at, got = project(512, m)
            if last:
                neigh[at, :] = got.astype(BF)
            else:
                acc[at, 512:] = got

        if not last:
            @pl.loop(0, 4)
            def _(m):
                at, got = project(0, m)
                acc[at, :512] = got

    def send_halo(layer, outgoing, halo):
        for g, dx in enumerate(STEPS):
            there_x = lax.rem(x + dx, 4)
            at = pl.ds(pl.multiple_of(there_x * 256, 256), 256)
            picked = dot(pick[at, :], neigh[...])
            outgoing[pl.ds(there_x * 32, 32)] = picked.reshape(32, 8, HID).astype(BF)

            @pl.loop(1 if dx == 0 else 0, 32)
            def _(i):
                there_dp = there_x * 2 + lax.rem(c + i % 2, 2)
                there_mp = lax.rem(y + i // 8, 4) * 4 + lax.rem(z + (i // 2) % 4, 4)
                remote(
                    outgoing.at[there_dp * 16 + there_mp], halo.at[dp * 16 + mp],
                    h_send.at[layer], h_recv.at[layer, g], (there_dp, there_mp),
                ).start()

        halo[dp * 16 + mp] = outgoing[dp * 16 + mp]

    def own(bias):
        @pl.loop(0, 4)
        def _(m):
            at = pl.ds(pl.multiple_of(m * 256, 256), 256)
            acc[at, :512] = acc[at, :512] + bias[...] + dot(adj[at, :ND], neigh[...])

    def receive_halo(layer, halo, finish):
        for g, dx in enumerate(STEPS):
            part = halo.at[pl.ds(0, 31 if dx == 0 else 32)]
            remote(part, part, h_send.at[layer], h_recv.at[layer, g], (dp, mp)).wait_recv()
            from_x = lax.rem(x + 4 - dx, 4)
            src = halo[pl.ds(from_x * 32, 32)].reshape(256, HID)
            cols = pl.ds(pl.multiple_of(ND + from_x * 256, 256), 256)

            @pl.loop(0, 4)
            def _(m):
                at = pl.ds(pl.multiple_of(m * 256, 256), 256)
                got = acc[at, :512] + dot(adj[at, cols], src)
                if g == 3:
                    finish(m, at, got)
                else:
                    acc[at, :512] = got

    send_halo(0, outgoing1, halo1)

    @pl.loop(0, 4)
    def _(m):
        at, got = project(0, m)
        acc[at, :512] = got

    own(bias1)

    def finish1(m, at, got):
        hidden[at, :] = jnp.maximum(got, 0.0).astype(BF)

    receive_halo(0, halo1, finish1)

    @pl.loop(0, 4)
    def _(m):
        at = pl.ds(pl.multiple_of(m * 256, 256), 256)
        neigh[at, :] = dot(hidden[at, :], w2v[:, 512:]).astype(BF)

    send_halo(1, outgoing2, halo2)

    @pl.loop(0, 4)
    def _(m):
        at = pl.ds(pl.multiple_of(m * 256, 256), 256)
        acc[at, :512] = dot(hidden[at, :], w2v[:, :512])

    own(bias2)

    def finish2(m, at, got):
        result[at, :] = got.astype(BF)
        pltpu.make_async_copy(result.at[at], out.at[at], o_sem.at[m]).start()

    receive_halo(1, halo2, finish2)

    for m in range(4):
        at = pl.ds(m * 256, 256)
        pltpu.make_async_copy(result.at[at], out.at[at], o_sem.at[m]).wait()

    sent = xt.at[pl.ds(0, 15)]
    remote(sent, sent, x_send, x_recv.at[0], (dp, mp)).wait_send()
    sent = w1f.at[pl.ds(0, 15), :, pl.ds(0, 128)]
    remote(sent, sent, w_send.at[0], w_recv.at[0], (dp, mp)).wait_send()
    remote(others, others, w_send.at[1], w_recv.at[1], (dp, mp)).wait_send()
    remote(half, half, w_send.at[2], w_recv.at[2], (dp, mp)).wait_send()
    for layer, outgoing in enumerate((outgoing1, outgoing2)):
        sent = outgoing.at[pl.ds(0, 127)]
        remote(sent, sent, h_send.at[layer], h_recv.at[layer, 0], (dp, mp)).wait_send()


def shards(
    features, weights1, bias1, weights2, bias2, send_rows, tile_dst, tile_src, tile_count, tile_vals
):
    pos = tile_dst[0] * 16 + tile_src[0]
    place = jnp.arange(128, dtype=jnp.int32)
    hit = (pos[None, :] == place[:, None]) & (place[None, :] < tile_count[0])
    slot = jnp.sum(jnp.where(hit, place[None, :] - 128, 0), axis=1) + 128

    hbm = pl.BlockSpec(memory_space=pl.ANY)
    vmem = pl.BlockSpec(memory_space=pltpu.VMEM)
    smem = pl.BlockSpec(memory_space=pltpu.SMEM)
    dma = pltpu.SemaphoreType.DMA
    return pl.pallas_call(
        kernel,
        out_shape=jax.ShapeDtypeStruct((ND, HID), BF),
        in_specs=[hbm, hbm, vmem, hbm, vmem, vmem, smem, hbm],
        out_specs=hbm,
        scratch_shapes=[
            pltpu.VMEM((16, 64, ND), BF),
            pltpu.VMEM((16, 64, 2 * HID), BF),
            pltpu.VMEM((HID, 2 * HID), BF),
            pltpu.VMEM((129, TILE, TILE), BF),
            pltpu.VMEM((ND, 2 * ND), BF),
            pltpu.VMEM((ND, ND), BF),
            pltpu.VMEM((ND, 2 * HID), F32),
            pltpu.VMEM((ND, HID), BF),
            pltpu.VMEM((ND, HID), BF),
            pltpu.VMEM((ND, HID), BF),
            pltpu.VMEM((128, 8, HID), BF),
            pltpu.VMEM((128, 8, HID), BF),
            pltpu.VMEM((128, 8, HID), BF),
            pltpu.VMEM((128, 8, HID), BF),
            dma((4,)), dma, dma((4,)), dma((3,)), dma((3,)), dma((2,)), dma((2, 4)), dma((4,)),
        ],
        compiler_params=pltpu.CompilerParams(
            collective_id=0, has_side_effects=True, vmem_limit_bytes=56 * 2**20
        ),
    )(
        features.T, weights1, bias1.reshape(1, HID), weights2, bias2.reshape(1, HID),
        send_rows[0].T, slot, tile_vals[0],
    )


def solution(mesh):
    return jax.shard_map(
        shards,
        mesh=mesh,
        in_specs=(
            P("dp", "mp"),
            P("mp", None),
            P(),
            P(),
            P(),
            P(("dp", "mp"), None, None),
            P(("dp", "mp"), None),
            P(("dp", "mp"), None),
            P(("dp", "mp")),
            P(("dp", "mp"), None, None, None),
        ),
        out_specs=P(("dp", "mp"), None),
        check_vma=False,
    )
```

time: 161 us -> 100 us (0.62)
  Pallas kernels: 0 us -> 95.6 us
  waiting for transfers between devices: 59.4 us -> 0 us
  blocking collectives: 23.1 us -> 0 us
  local copies, waits for them, and re-layouts: 21.6 us -> 2.26 us
  matrix products: 18.5 us -> 0 us
  starting transfers between devices: 17.2 us -> 0 us
  between operations: 14.2 us -> 0.67 us
  other arithmetic: 6.88 us -> 1.32 us
    pallas_call x0 -> x1, Pallas kernels: none -> 95.6 us  [shards(): pl.pallas_call(kernel, out_shape=jax.ShapeDtypeStruct((ND, HID), BF), in_...]
    all_to_all x2 -> x0, waiting for transfers between devices: 35.8 us -> none  [the longest x1 29.1 us: shards(): lax.all_to_all(features.reshape(16, ND, 64), 'mp', split_axis=0, concat_a...]
    all_to_all x1 -> x0, blocking collectives: 23.1 us -> none  [layer(): lax.all_to_all(outgoing, ('dp', 'mp'), split_axis=0, concat_axis=0, tiled...]
    all_gather x1 -> x0, waiting for transfers between devices: 22.9 us -> none  [shards(): w1 = lax.all_gather(weights1, 'mp', axis=0, tiled=True)]
    dot_general x3 -> x0, matrix products: 18.5 us -> none  [the longest x1 8.27 us: shards(): proj2 = jnp.dot(hidden1, weights2, preferred_element_type=jnp.float32)]
    all_to_all x2 -> x0, starting transfers between devices: 17.2 us -> none  [the longest x1 8.6 us: shards(): lax.all_to_all(features.reshape(16, ND, 64), 'mp', split_axis=0, concat_a...]
    gather x3 -> x0, local copies, waits for them, and re-layouts: 14.3 us -> none  [the longest x2 9.05 us: layer(): outgoing = neigh[rows].reshape(128, 8, 512)]
    select_n x3 -> x0, other arithmetic: 6.63 us -> none  [the longest x2 6.62 us: dense_adjacency(): tiles = jnp.where(live[:, None, None], vals[inv], 0)]
  transfers between devices with their start and end apart: 3 -> 0, of which waited for: 3 -> 0; matrix products, arithmetic and copies ran while one was open for 10% -> 0% of each run, Pallas kernels for 0% -> 0%
where the time goes in v2:
time: 100 us; the launch traced here: 99.8 us
  Pallas kernels  95.6 us (96%)
  local copies, waits for them, and re-layouts  2.26 us (2%)
  other arithmetic  1.32 us (1%)
    pallas_call x1, Pallas kernels, shards(): pl.pallas_call(kernel, out_shape=jax.ShapeDtypeStruct((ND, HID), BF), in_...  95.6 us
    unnamed x1, local copies, waits for them, and re-layouts  2.26 us

profile of v2, /device:TPU:1, one launch (start us, length us, event | category | flops | bytes accessed | tf_op | source)
XLA Modules:
  0.0 99.8 jit_solution(18149562486474090479)
XLA Ops:
  0.7 0.7 add_bitcast_fusion
  1.3 0.1 select_reduce_fusion
  1.5 0.5 broadcast_add_fusion.slot
  2.0 95.6 %shard_map.100 = bf16[1024,512]{1,0:T(8,128)(2,1)} custom-call(bf16[64,16384]{1,0:T(8,128)(2,1)} %bitcast.12, bf16[64,1024]{1,0:T(8,128)(2,1)} %w1.1, f32[1,512]{1,0:T(1,128)} %bitcast.14, bf16[512,1024]{1,0:T(8,128)(2,1)} %w2.1, f32[1,512]{1,0:T(1,128)} %bitcast.15, s32[8,128]{1,0:T(8,128)} %bitcast.13, s32[128]{0:T(128)} %broadcast_add_fusion.slot, ...), custom_call_target="tpu_custom_call" | custom-call | tf_op jit(solution)/shard_map/pallas_call | solution.py:236
  97.6 2.3 %copy.13 = bf16[1024,512]{1,0:T(8,128)(2,1)} copy(bf16[1024,512]{1,0:T(8,128)(2,1)} %shard_map.100) | data formatting | bytes 2097152
  (2 shorter events, 0.0 us)

commit v3 on v2

v3 whole, which is shorter than its diff:
```python
import jax
import jax.numpy as jnp
from jax import lax
from jax.experimental import pallas as pl
from jax.experimental.pallas import tpu as pltpu
from jax.sharding import PartitionSpec as P

MESH = pl.DeviceIdType.MESH
ND, F, HID, TILE = 1024, 1024, 512, 128
STEPS = (2, 1, 3, 0)
PLANE = ((2, 2), (2, 1), (1, 2), (2, 3), (3, 2), (0, 2), (2, 0), (1, 1), (3, 3), (1, 3), (3, 1), (0, 1), (1, 0), (0, 3), (3, 0))
BF = jnp.bfloat16
F32 = jnp.float32


def dot(a, b):
    return jnp.dot(a, b, preferred_element_type=F32)


def dot_t(a, b):
    return lax.dot_general(a, b, (((0,), (0,)), ((), ())), preferred_element_type=F32)


def dot_nt(a, b):
    return lax.dot_general(a, b, (((1,), (1,)), ((), ())), preferred_element_type=F32)


def kernel(
    feat, w1, bias1, w2, bias2, rows, dst, src_tile, count, vals, out,
    xs, xt, w1f, w1t, w2v, tiles, adj, pick, acc, acc_t, neigh_t, neigh, hidden, result, slot_v, slot,
    outgoing1, outgoing2, halo1, halo2,
    local_sem, x_send, x_recv, w_send, w_recv, h_send, h_recv, o_sem,
):
    dp, mp = lax.axis_index("dp"), lax.axis_index("mp")
    x, c, y, z = dp // 2, dp % 2, mp // 4, mp % 4
    xs_at = [lax.rem(x + d, 4) for d in range(4)]
    ys_at = [lax.rem(y + d, 4) * 4 for d in range(4)]
    zs_at = [lax.rem(z + d, 4) for d in range(4)]
    cs_at = [c, 1 - c]

    def remote(src, dst, send, recv, to):
        return pltpu.make_async_remote_copy(
            src_ref=src, dst_ref=dst, send_sem=send, recv_sem=recv, device_id=to, device_id_type=MESH
        )

    barrier = pltpu.get_barrier_semaphore()
    plane = [ys_at[a] + zs_at[b] for a, b in PLANE]
    along_x = [(xs_at[d] * 2 + c, mp) for d in (1, 3, 2)]
    sibling = x * 2 + 1 - c, mp
    for there in [(dp, p) for p in plane] + along_x + [sibling]:
        pl.semaphore_signal(barrier, inc=1, device_id=there, device_id_type=MESH)

    cb = pl.multiple_of((c * 4 + x) * 128, 128)
    w1_mine = pltpu.make_async_copy(w1.at[:, pl.ds(cb, 128)], w1f.at[mp, :, pl.ds(cb, 128)], local_sem.at[0])
    w1_mine.start()
    staged = [
        pltpu.make_async_copy(feat.at[:, pl.ds(p * ND, ND)], xs.at[p], local_sem.at[1]) for p in range(16)
    ]
    for copy in staged:
        copy.start()
    tiles_in = pltpu.make_async_copy(vals, tiles.at[pl.ds(0, 128)], local_sem.at[2])
    tiles_in.start()
    w2_in = pltpu.make_async_copy(w2, w2v, local_sem.at[3])
    w2_in.start()

    place = jnp.broadcast_to(dst[...] * 16 + src_tile[...], (128, 128)).T
    t_iota = lax.broadcasted_iota(jnp.int32, (128, 128), 0)
    q_iota = lax.broadcasted_iota(jnp.int32, (128, 128), 1)
    hit = (place == q_iota) & (t_iota < count[0])
    slot_v[...] = jnp.sum(jnp.where(hit, t_iota - 128, 0), axis=0, keepdims=True) + 128
    slot_in = pltpu.make_async_copy(slot_v, slot, local_sem.at[4])
    slot_in.start()
    tiles[128] = jnp.zeros((TILE, TILE), BF)

    table = rows[...]
    lanes = lax.broadcasted_iota(jnp.int32, (16, ND), 1)
    for r in range(0, 128, 2):
        want = jnp.concatenate([table[:, r : r + 1], table[:, r + 1 : r + 2]], axis=0)
        pick[r * 8 : r * 8 + 16, :] = jnp.where(want == lanes, 1.0, 0.0).astype(BF)

    pltpu.make_async_copy(xs, xs, local_sem.at[1]).wait()
    pl.semaphore_wait(barrier, 19)

    for p in plane:
        remote(
            w1.at[:, pl.ds(cb, 128)], w1f.at[mp, :, pl.ds(cb, 128)], w_send.at[0], w_recv.at[0], (dp, p)
        ).start()

    for (a, b), p in zip(PLANE, plane):
        remote(xs.at[p], xt.at[mp], x_send, x_recv.at[STEPS.index(a)], (dp, p)).start()
    xt_mine = pltpu.make_async_copy(xs.at[mp], xt.at[mp], local_sem.at[5])
    xt_mine.start()

    w1_mine.wait()
    got = w1f.at[pl.ds(0, 15), :, pl.ds(0, 128)]
    remote(got, got, w_send.at[0], w_recv.at[0], (dp, mp)).wait_recv()
    for there in along_x:
        part = w1f.at[:, :, pl.ds(cb, 128)]
        remote(part, part, w_send.at[1], w_recv.at[1], there).start()

    tiles_in.wait()
    slot_in.wait()

    @pl.loop(0, 8)
    def _(d):
        at = pl.ds(pl.multiple_of(d * TILE, TILE), TILE)
        for s in range(16):
            adj[at, s * TILE : (s + 1) * TILE] = tiles[slot[0, d * 16 + s]]

    others = w1f.at[:, :, pl.ds(0, 384)]
    remote(others, others, w_send.at[1], w_recv.at[1], (dp, mp)).wait_recv()
    half = w1f.at[:, :, pl.ds(pl.multiple_of(c * 512, 512), 512)]
    remote(half, half, w_send.at[2], w_recv.at[2], sibling).start()
    remote(half, half, w_send.at[2], w_recv.at[2], (dp, mp)).wait_recv()
    for k in range(4):
        w1t[:, k * 256 : (k + 1) * 256] = w1f[k * 4 : k * 4 + 4, :, 512:].reshape(256, HID).T
    w2_in.wait()
    xt_mine.wait()

    for g, dy in enumerate(STEPS):
        part = xt.at[pl.ds(0, 3 if dy == 0 else 4)]
        remote(part, part, x_send, x_recv.at[g], (dp, mp)).wait_recv()
        from_y = lax.rem(y + 4 - dy, 4)
        weights = w1t[:, pl.ds(pl.multiple_of(from_y * 256, 256), 256)]
        for n in range(0, ND, 512):
            add = dot(weights, xt[pl.ds(from_y * 4, 4), :, n : n + 512].reshape(256, 512))
            if g > 0:
                add = add + acc_t[:, n : n + 512]
            if g < 3:
                acc_t[:, n : n + 512] = add
            else:
                neigh_t[:, n : n + 512] = add.astype(BF)

    def send_halo(layer, picked, outgoing, halo):
        for g, dx in enumerate(STEPS):
            there_x = xs_at[dx]
            at = pl.ds(pl.multiple_of(there_x * 256, 256), 256)
            outgoing[pl.ds(there_x * 32, 32)] = picked(pick[at, :]).reshape(32, 8, HID).astype(BF)
            for a in STEPS:
                for b in STEPS:
                    for e in (1, 0):
                        if (dx, a, b, e) != (0, 0, 0, 0):
                            there_dp, there_mp = there_x * 2 + cs_at[e], ys_at[a] + zs_at[b]
                            remote(
                                outgoing.at[there_dp * 16 + there_mp], halo.at[dp * 16 + mp],
                                h_send.at[layer], h_recv.at[layer, g], (there_dp, there_mp),
                            ).start()
        halo[dp * 16 + mp] = outgoing[dp * 16 + mp]

    def receive_halo(layer, halo, project, finish):
        for g, dx in enumerate(STEPS):
            part = halo.at[pl.ds(0, 31 if dx == 0 else 32)]
            remote(part, part, h_send.at[layer], h_recv.at[layer, g], (dp, mp)).wait_recv()
            from_x = lax.rem(x + 4 - dx, 4)
            src = project(halo[pl.ds(from_x * 32, 32)].reshape(256, HID))
            cols = pl.ds(pl.multiple_of(ND + from_x * 256, 256), 256)
            for m in range(2):
                at = pl.ds(m * 512, 512)
                add = acc[at, :] + dot(adj[at, cols], src)
                if g == 3:
                    finish(m, at, add)
                else:
                    acc[at, :] = add

    send_halo(0, lambda one_hot: dot_nt(one_hot, neigh_t[...]), outgoing1, halo1)

    @pl.loop(0, 4)
    def _(m):
        at = pl.ds(pl.multiple_of(m * 256, 256), 256)
        self_part = dot_t(xt[:, :, at].reshape(ND, 256), w1f[:, :, :512].reshape(F, HID))
        acc[at, :] = self_part + bias1[...] + dot_nt(adj[at, :ND], neigh_t[...])

    def finish1(m, at, add):
        hidden[at, :] = jnp.maximum(add, 0.0).astype(BF)

    receive_halo(0, halo1, lambda block: block, finish1)

    send_halo(1, lambda one_hot: dot(one_hot, hidden[...]), outgoing2, halo2)

    @pl.loop(0, 4)
    def _(m):
        at = pl.ds(pl.multiple_of(m * 256, 256), 256)
        neigh[at, :] = dot(hidden[at, :], w2v[:, 512:]).astype(BF)

    @pl.loop(0, 4)
    def _(m):
        at = pl.ds(pl.multiple_of(m * 256, 256), 256)
        acc[at, :] = dot(hidden[at, :], w2v[:, :512]) + bias2[...] + dot(adj[at, :ND], neigh[...])

    def finish2(m, at, add):
        result[at, :] = add.astype(BF)
        pltpu.make_async_copy(result.at[at], out.at[at], o_sem.at[m]).start()

    receive_halo(1, halo2, lambda block: dot(block, w2v[:, 512:]).astype(BF), finish2)
    for m in range(2):
        at = pl.ds(m * 512, 512)
        pltpu.make_async_copy(result.at[at], out.at[at], o_sem.at[m]).wait()

    sent = xt.at[pl.ds(0, 15)]
    remote(sent, sent, x_send, x_recv.at[0], (dp, mp)).wait_send()
    remote(got, got, w_send.at[0], w_recv.at[0], (dp, mp)).wait_send()
    remote(others, others, w_send.at[1], w_recv.at[1], (dp, mp)).wait_send()
    remote(half, half, w_send.at[2], w_recv.at[2], (dp, mp)).wait_send()
    for layer, outgoing in enumerate((outgoing1, outgoing2)):
        sent = outgoing.at[pl.ds(0, 127)]
        remote(sent, sent, h_send.at[layer], h_recv.at[layer, 0], (dp, mp)).wait_send()


def shards(
    features, weights1, bias1, weights2, bias2, send_rows, tile_dst, tile_src, tile_count, tile_vals
):
    hbm = pl.BlockSpec(memory_space=pl.ANY)
    vmem = pl.BlockSpec(memory_space=pltpu.VMEM)
    smem = pl.BlockSpec(memory_space=pltpu.SMEM)
    dma = pltpu.SemaphoreType.DMA
    return pl.pallas_call(
        kernel,
        out_shape=jax.ShapeDtypeStruct((ND, HID), BF),
        in_specs=[hbm, hbm, vmem, hbm, vmem, vmem, vmem, vmem, smem, hbm],
        out_specs=hbm,
        scratch_shapes=[
            pltpu.VMEM((16, 64, ND), BF),
            pltpu.VMEM((16, 64, ND), BF),
            pltpu.VMEM((16, 64, 2 * HID), BF),
            pltpu.VMEM((HID, F), BF),
            pltpu.VMEM((HID, 2 * HID), BF),
            pltpu.VMEM((129, TILE, TILE), BF),
            pltpu.VMEM((ND, 2 * ND), BF),
            pltpu.VMEM((ND, ND), BF),
            pltpu.VMEM((ND, HID), F32),
            pltpu.VMEM((HID, ND), F32),
            pltpu.VMEM((HID, ND), BF),
            pltpu.VMEM((ND, HID), BF),
            pltpu.VMEM((ND, HID), BF),
            pltpu.VMEM((ND, HID), BF),
            pltpu.VMEM((1, 128), jnp.int32),
            pltpu.SMEM((1, 128), jnp.int32),
            pltpu.VMEM((128, 8, HID), BF),
            pltpu.VMEM((128, 8, HID), BF),
            pltpu.VMEM((128, 8, HID), BF),
            pltpu.VMEM((128, 8, HID), BF),
            dma((6,)), dma, dma((4,)), dma((3,)), dma((3,)), dma((2,)), dma((2, 4)), dma((2,)),
        ],
        compiler_params=pltpu.CompilerParams(
            collective_id=0, has_side_effects=True, vmem_limit_bytes=56 * 2**20
        ),
    )(
        features.T, weights1, bias1.reshape(1, HID), weights2, bias2.reshape(1, HID),
        send_rows[0].T, tile_dst, tile_src, tile_count, tile_vals[0],
    )


def solution(mesh):
    return jax.shard_map(
        shards,
        mesh=mesh,
        in_specs=(
            P("dp", "mp"),
            P("mp", None),
            P(),
            P(),
            P(),
            P(("dp", "mp"), None, None),
            P(("dp", "mp"), None),
            P(("dp", "mp"), None),
            P(("dp", "mp")),
            P(("dp", "mp"), None, None, None),
        ),
        out_specs=P(("dp", "mp"), None),
        check_vma=False,
    )
```

time: 100 us -> 81.8 us (0.82)
  Pallas kernels: 95.6 us -> 78.7 us
  other arithmetic: 1.32 us -> 0 us
    pallas_call x1, Pallas kernels: 95.6 us -> 78.7 us  [shards(): pl.pallas_call(kernel, out_shape=jax.ShapeDtypeStruct((ND, HID), BF), in_...]
where the time goes in v3:
time: 81.8 us; the launch traced here: 81.6 us
  Pallas kernels  78.7 us (96%)
  local copies, waits for them, and re-layouts  2.26 us (3%)
    pallas_call x1, Pallas kernels, shards(): pl.pallas_call(kernel, out_shape=jax.ShapeDtypeStruct((ND, HID), BF), in_...  78.7 us
    unnamed x1, local copies, waits for them, and re-layouts  2.26 us

profile of v3, /device:TPU:1, one launch (start us, length us, event | category | flops | bytes accessed | tf_op | source)
XLA Modules:
  0.0 81.6 jit_solution(4227023511308926412)
XLA Ops:
  0.7 78.7 %shard_map.100 = bf16[1024,512]{1,0:T(8,128)(2,1)} custom-call(bf16[64,16384]{1,0:T(8,128)(2,1)} %bitcast.8, bf16[64,1024]{1,0:T(8,128)(2,1)} %w1.1, f32[1,512]{1,0:T(1,128)} %bitcast.10, bf16[512,1024]{1,0:T(8,128)(2,1)} %w2.1, f32[1,512]{1,0:T(1,128)} %bitcast.11, s32[8,128]{1,0:T(8,128)} %bitcast.9, s32[1,128]{1,0:T(1,128)} %dst.1, s32[1,128]{1,0:T(1,128)} %src_tile.1, ...), custom_call_target="tpu_custom_call" | custom-call | tf_op jit(solution)/shard_map/pallas_call | solution.py:216
  79.4 2.3 %copy.13 = bf16[1024,512]{1,0:T(8,128)(2,1)} copy(bf16[1024,512]{1,0:T(8,128)(2,1)} %shard_map.100) | data formatting | bytes 2097152

commit v4 on v3

--- a/solution.py
+++ b/solution.py
@@ -27,7 +27,7 @@
 
 def kernel(
     feat, w1, bias1, w2, bias2, rows, dst, src_tile, count, vals, out,
-    xs, xt, w1f, w1t, w2v, tiles, adj, pick, acc, acc_t, neigh_t, neigh, hidden, result, slot_v, slot,
+    xs, xt, w1f, w1t, w1s, w2v, tiles, adj, pick, acc, acc_t, neigh_t, neigh, hidden, result, slot_v, slot,
     outgoing1, outgoing2, halo1, halo2,
     local_sem, x_send, x_recv, w_send, w_recv, h_send, h_recv, o_sem,
 ):
@@ -50,17 +50,24 @@
     for there in [(dp, p) for p in plane] + along_x + [sibling]:
         pl.semaphore_signal(barrier, inc=1, device_id=there, device_id_type=MESH)
 
-    cb = pl.multiple_of((c * 4 + x) * 128, 128)
-    w1_mine = pltpu.make_async_copy(w1.at[:, pl.ds(cb, 128)], w1f.at[mp, :, pl.ds(cb, 128)], local_sem.at[0])
-    w1_mine.start()
+    w_rows = pl.ds(pl.multiple_of(c * 32, 32), 32)
+    w1_mine = [
+        pltpu.make_async_copy(
+            w1.at[w_rows, pl.ds(pl.multiple_of(h * HID + x * 128, 128), 128)],
+            w1f.at[h, c, x, mp], local_sem.at[0, h],
+        )
+        for h in range(2)
+    ]
+    for copy in w1_mine:
+        copy.start()
     staged = [
-        pltpu.make_async_copy(feat.at[:, pl.ds(p * ND, ND)], xs.at[p], local_sem.at[1]) for p in range(16)
+        pltpu.make_async_copy(feat.at[:, pl.ds(p * ND, ND)], xs.at[p], local_sem.at[1, 0]) for p in range(16)
     ]
     for copy in staged:
         copy.start()
-    tiles_in = pltpu.make_async_copy(vals, tiles.at[pl.ds(0, 128)], local_sem.at[2])
+    tiles_in = pltpu.make_async_copy(vals, tiles.at[pl.ds(0, 128)], local_sem.at[2, 0])
     tiles_in.start()
-    w2_in = pltpu.make_async_copy(w2, w2v, local_sem.at[3])
+    w2_in = pltpu.make_async_copy(w2, w2v, local_sem.at[3, 0])
     w2_in.start()
 
     place = jnp.broadcast_to(dst[...] * 16 + src_tile[...], (128, 128)).T
@@ -68,7 +75,7 @@
     q_iota = lax.broadcasted_iota(jnp.int32, (128, 128), 1)
     hit = (place == q_iota) & (t_iota < count[0])
     slot_v[...] = jnp.sum(jnp.where(hit, t_iota - 128, 0), axis=0, keepdims=True) + 128
-    slot_in = pltpu.make_async_copy(slot_v, slot, local_sem.at[4])
+    slot_in = pltpu.make_async_copy(slot_v, slot, local_sem.at[4, 0])
     slot_in.start()
     tiles[128] = jnp.zeros((TILE, TILE), BF)
 
@@ -78,25 +85,29 @@
         want = jnp.concatenate([table[:, r : r + 1], table[:, r + 1 : r + 2]], axis=0)
         pick[r * 8 : r * 8 + 16, :] = jnp.where(want == lanes, 1.0, 0.0).astype(BF)
 
-    pltpu.make_async_copy(xs, xs, local_sem.at[1]).wait()
+    pltpu.make_async_copy(xs, xs, local_sem.at[1, 0]).wait()
     pl.semaphore_wait(barrier, 19)
 
-    for p in plane:
-        remote(
-            w1.at[:, pl.ds(cb, 128)], w1f.at[mp, :, pl.ds(cb, 128)], w_send.at[0], w_recv.at[0], (dp, p)
-        ).start()
+    for h in (1, 0):
+        w1_mine[h].wait()
+        for p in plane:
+            block = w1f.at[h, c, x, mp]
+            remote(block, block, w_send.at[0, h], w_recv.at[0, h], (dp, p)).start()
 
     for (a, b), p in zip(PLANE, plane):
         remote(xs.at[p], xt.at[mp], x_send, x_recv.at[STEPS.index(a)], (dp, p)).start()
-    xt_mine = pltpu.make_async_copy(xs.at[mp], xt.at[mp], local_sem.at[5])
+    xt_mine = pltpu.make_async_copy(xs.at[mp], xt.at[mp], local_sem.at[5, 0])
     xt_mine.start()
 
-    w1_mine.wait()
-    got = w1f.at[pl.ds(0, 15), :, pl.ds(0, 128)]
-    remote(got, got, w_send.at[0], w_recv.at[0], (dp, mp)).wait_recv()
-    for there in along_x:
-        part = w1f.at[:, :, pl.ds(cb, 128)]
-        remote(part, part, w_send.at[1], w_recv.at[1], there).start()
+    def w1_phase(phase, h):
+        part = (w1f.at[h, c, x, pl.ds(0, 15)], w1f.at[h, c, pl.ds(0, 3)], w1f.at[h, c])[phase]
+        return remote(part, part, w_send.at[phase, h], w_recv.at[phase, h], (dp, mp))
+
+    for h in (1, 0):
+        w1_phase(0, h).wait_recv()
+        for there in along_x:
+            part = w1f.at[h, c, x]
+            remote(part, part, w_send.at[1, h], w_recv.at[1, h], there).start()
 
     tiles_in.wait()
     slot_in.wait()
@@ -107,13 +118,16 @@
         for s in range(16):
             adj[at, s * TILE : (s + 1) * TILE] = tiles[slot[0, d * 16 + s]]
 
-    others = w1f.at[:, :, pl.ds(0, 384)]
-    remote(others, others, w_send.at[1], w_recv.at[1], (dp, mp)).wait_recv()
-    half = w1f.at[:, :, pl.ds(pl.multiple_of(c * 512, 512), 512)]
-    remote(half, half, w_send.at[2], w_recv.at[2], sibling).start()
-    remote(half, half, w_send.at[2], w_recv.at[2], (dp, mp)).wait_recv()
+    for h in (1, 0):
+        w1_phase(1, h).wait_recv()
+        remote(w1f.at[h, c], w1f.at[h, c], w_send.at[2, h], w_recv.at[2, h], sibling).start()
+
+    def w1_columns(h, k):
+        return w1f[h, :, k].swapaxes(0, 1).reshape(F, 128)
+
+    w1_phase(2, 1).wait_recv()
     for k in range(4):
-        w1t[:, k * 256 : (k + 1) * 256] = w1f[k * 4 : k * 4 + 4, :, 512:].reshape(256, HID).T
+        w1t[k * 128 : (k + 1) * 128, :] = w1_columns(1, k).T
     w2_in.wait()
     xt_mine.wait()
 
@@ -164,10 +178,14 @@
 
     send_halo(0, lambda one_hot: dot_nt(one_hot, neigh_t[...]), outgoing1, halo1)
 
+    w1_phase(2, 0).wait_recv()
+    for k in range(4):
+        w1s[:, k * 128 : (k + 1) * 128] = w1_columns(0, k)
+
     @pl.loop(0, 4)
     def _(m):
         at = pl.ds(pl.multiple_of(m * 256, 256), 256)
-        self_part = dot_t(xt[:, :, at].reshape(ND, 256), w1f[:, :, :512].reshape(F, HID))
+        self_part = dot_t(xt[:, :, at].reshape(ND, 256), w1s[...])
         acc[at, :] = self_part + bias1[...] + dot_nt(adj[at, :ND], neigh_t[...])
 
     def finish1(m, at, add):
@@ -198,9 +216,9 @@
 
     sent = xt.at[pl.ds(0, 15)]
     remote(sent, sent, x_send, x_recv.at[0], (dp, mp)).wait_send()
-    remote(got, got, w_send.at[0], w_recv.at[0], (dp, mp)).wait_send()
-    remote(others, others, w_send.at[1], w_recv.at[1], (dp, mp)).wait_send()
-    remote(half, half, w_send.at[2], w_recv.at[2], (dp, mp)).wait_send()
+    for phase in range(3):
+        for h in range(2):
+            w1_phase(phase, h).wait_send()
     for layer, outgoing in enumerate((outgoing1, outgoing2)):
         sent = outgoing.at[pl.ds(0, 127)]
         remote(sent, sent, h_send.at[layer], h_recv.at[layer, 0], (dp, mp)).wait_send()
@@ -221,8 +239,9 @@
         scratch_shapes=[
             pltpu.VMEM((16, 64, ND), BF),
             pltpu.VMEM((16, 64, ND), BF),
-            pltpu.VMEM((16, 64, 2 * HID), BF),
+            pltpu.VMEM((2, 2, 4, 16, 32, 128), BF),
             pltpu.VMEM((HID, F), BF),
+            pltpu.VMEM((F, HID), BF),
             pltpu.VMEM((HID, 2 * HID), BF),
             pltpu.VMEM((129, TILE, TILE), BF),
             pltpu.VMEM((ND, 2 * ND), BF),
@@ -239,7 +258,7 @@
             pltpu.VMEM((128, 8, HID), BF),
             pltpu.VMEM((128, 8, HID), BF),
             pltpu.VMEM((128, 8, HID), BF),
-            dma((6,)), dma, dma((4,)), dma((3,)), dma((3,)), dma((2,)), dma((2, 4)), dma((2,)),
+            dma((6, 2)), dma, dma((4,)), dma((3, 2)), dma((3, 2)), dma((2,)), dma((2, 4)), dma((2,)),
         ],
         compiler_params=pltpu.CompilerParams(
             collective_id=0, has_side_effects=True, vmem_limit_bytes=56 * 2**20

time: 81.8 us -> 75.8 us (0.927)
  Pallas kernels: 78.7 us -> 72.7 us
    pallas_call x1, Pallas kernels: 78.7 us -> 72.7 us  [shards(): pl.pallas_call(kernel, out_shape=jax.ShapeDtypeStruct((ND, HID), BF), in_...]
where the time goes in v4:
time: 75.8 us; the launch traced here: 75.6 us
  Pallas kernels  72.7 us (96%)
  local copies, waits for them, and re-layouts  2.26 us (3%)
    pallas_call x1, Pallas kernels, shards(): pl.pallas_call(kernel, out_shape=jax.ShapeDtypeStruct((ND, HID), BF), in_...  72.7 us
    unnamed x1, local copies, waits for them, and re-layouts  2.26 us

profile of v4, /device:TPU:1, one launch (start us, length us, event | category | flops | bytes accessed | tf_op | source)
XLA Modules:
  0.0 75.6 jit_solution(13317360564612530360)
XLA Ops:
  0.7 72.7 %shard_map.100 = bf16[1024,512]{1,0:T(8,128)(2,1)} custom-call(bf16[64,16384]{1,0:T(8,128)(2,1)} %bitcast.8, bf16[64,1024]{1,0:T(8,128)(2,1)} %w1.1, f32[1,512]{1,0:T(1,128)} %bitcast.10, bf16[512,1024]{1,0:T(8,128)(2,1)} %w2.1, f32[1,512]{1,0:T(1,128)} %bitcast.11, s32[8,128]{1,0:T(8,128)} %bitcast.9, s32[1,128]{1,0:T(1,128)} %dst.1, s32[1,128]{1,0:T(1,128)} %src_tile.1, ...), custom_call_target="tpu_custom_call" | custom-call | tf_op jit(solution)/shard_map/pallas_call | solution.py:234
  73.3 2.3 %copy.13 = bf16[1024,512]{1,0:T(8,128)(2,1)} copy(bf16[1024,512]{1,0:T(8,128)(2,1)} %shard_map.100) | data formatting | bytes 2097152

commit v5 on v4

--- a/solution.py
+++ b/solution.py
@@ -27,9 +27,9 @@
 
 def kernel(
     feat, w1, bias1, w2, bias2, rows, dst, src_tile, count, vals, out,
-    xs, xt, w1f, w1t, w1s, w2v, tiles, adj, pick, acc, acc_t, neigh_t, neigh, hidden, result, slot_v, slot,
-    outgoing1, outgoing2, halo1, halo2,
-    local_sem, x_send, x_recv, w_send, w_recv, h_send, h_recv, o_sem,
+    xs, xt, w1f, w1t, w1s, w2v, tiles, adj, pick, acc, acc_t, neigh_t, neigh, hidden, part2, slot_v, slot,
+    stage, halo,
+    local_sem, x_send, x_recv, w_send, w_recv, h_send, h_recv,
 ):
     dp, mp = lax.axis_index("dp"), lax.axis_index("mp")
     x, c, y, z = dp // 2, dp % 2, mp // 4, mp % 4
@@ -136,92 +136,108 @@
         remote(part, part, x_send, x_recv.at[g], (dp, mp)).wait_recv()
         from_y = lax.rem(y + 4 - dy, 4)
         weights = w1t[:, pl.ds(pl.multiple_of(from_y * 256, 256), 256)]
-        for n in range(0, ND, 512):
-            add = dot(weights, xt[pl.ds(from_y * 4, 4), :, n : n + 512].reshape(256, 512))
-            if g > 0:
-                add = add + acc_t[:, n : n + 512]
-            if g < 3:
-                acc_t[:, n : n + 512] = add
-            else:
-                neigh_t[:, n : n + 512] = add.astype(BF)
-
-    def send_halo(layer, picked, outgoing, halo):
+        if g < 3:
+            for n in range(0, ND, 512):
+                add = dot(weights, xt[pl.ds(from_y * 4, 4), :, n : n + 512].reshape(256, 512))
+                acc_t[:, n : n + 512] = add if g == 0 else add + acc_t[:, n : n + 512]
+
+    def neighbours(h):
+        at = pl.ds(h * 256, 256)
+        neigh_t[at, :] = (
+            acc_t[at, :] + dot(w1t[at, pl.ds(pl.multiple_of(y * 256, 256), 256)], xt[pl.ds(y * 4, 4)].reshape(256, ND))
+        ).astype(BF)
+
+    def send_rows(layer, h, picked):
         for g, dx in enumerate(STEPS):
-            there_x = xs_at[dx]
-            at = pl.ds(pl.multiple_of(there_x * 256, 256), 256)
-            outgoing[pl.ds(there_x * 32, 32)] = picked(pick[at, :]).reshape(32, 8, HID).astype(BF)
+            at = pl.ds(pl.multiple_of(xs_at[dx] * 256, 256), 256)
+            stage[layer, h, pl.ds(xs_at[dx] * 32, 32)] = picked(pick[at, :]).reshape(32, 8, 256).astype(BF)
             for a in STEPS:
                 for b in STEPS:
                     for e in (1, 0):
                         if (dx, a, b, e) != (0, 0, 0, 0):
-                            there_dp, there_mp = there_x * 2 + cs_at[e], ys_at[a] + zs_at[b]
+                            there_dp, there_mp = xs_at[dx] * 2 + cs_at[e], ys_at[a] + zs_at[b]
                             remote(
-                                outgoing.at[there_dp * 16 + there_mp], halo.at[dp * 16 + mp],
-                                h_send.at[layer], h_recv.at[layer, g], (there_dp, there_mp),
+                                stage.at[layer, h, there_dp * 16 + there_mp], halo.at[layer, h, dp * 16 + mp],
+                                h_send.at[layer, h], h_recv.at[layer, h, g], (there_dp, there_mp),
                             ).start()
-        halo[dp * 16 + mp] = outgoing[dp * 16 + mp]
-
-    def receive_halo(layer, halo, project, finish):
-        for g, dx in enumerate(STEPS):
-            part = halo.at[pl.ds(0, 31 if dx == 0 else 32)]
-            remote(part, part, h_send.at[layer], h_recv.at[layer, g], (dp, mp)).wait_recv()
-            from_x = lax.rem(x + 4 - dx, 4)
-            src = project(halo[pl.ds(from_x * 32, 32)].reshape(256, HID))
-            cols = pl.ds(pl.multiple_of(ND + from_x * 256, 256), 256)
-            for m in range(2):
-                at = pl.ds(m * 512, 512)
-                add = acc[at, :] + dot(adj[at, cols], src)
-                if g == 3:
-                    finish(m, at, add)
-                else:
-                    acc[at, :] = add
-
-    send_halo(0, lambda one_hot: dot_nt(one_hot, neigh_t[...]), outgoing1, halo1)
-
+        halo[layer, h, dp * 16 + mp] = stage[layer, h, dp * 16 + mp]
+
+    def arrived(layer, h, g):
+        part = halo.at[layer, h, pl.ds(0, 31 if g == 3 else 32)]
+        remote(part, part, h_send.at[layer, h], h_recv.at[layer, h, g], (dp, mp)).wait_recv()
+        from_x = lax.rem(x + 4 - STEPS[g], 4)
+        return (
+            halo[layer, h, pl.ds(from_x * 32, 32)].reshape(256, 256),
+            pl.ds(pl.multiple_of(ND + from_x * 256, 256), 256),
+            pl.ds(pl.multiple_of(from_x * 256, 256), 256),
+        )
+
+    def own1(h):
+        half = pl.ds(h * 256, 256)
+
+        @pl.loop(0, 2)
+        def _(m):
+            at = pl.ds(pl.multiple_of(m * 512, 512), 512)
+            self_part = dot_t(xt[:, :, at].reshape(F, 512), w1s[:, half])
+            acc[at, half] = self_part + bias1[:, half] + dot_nt(adj[at, :ND], neigh_t[half, :])
+
+    def picked1(h):
+        return lambda one_hot: dot_nt(one_hot, neigh_t[h * 256 : (h + 1) * 256, :])
+
+    neighbours(0)
+    send_rows(0, 0, picked1(0))
+    neighbours(1)
+    send_rows(0, 1, picked1(1))
     w1_phase(2, 0).wait_recv()
     for k in range(4):
         w1s[:, k * 128 : (k + 1) * 128] = w1_columns(0, k)
-
-    @pl.loop(0, 4)
-    def _(m):
-        at = pl.ds(pl.multiple_of(m * 256, 256), 256)
-        self_part = dot_t(xt[:, :, at].reshape(ND, 256), w1s[...])
-        acc[at, :] = self_part + bias1[...] + dot_nt(adj[at, :ND], neigh_t[...])
-
-    def finish1(m, at, add):
-        hidden[at, :] = jnp.maximum(add, 0.0).astype(BF)
-
-    receive_halo(0, halo1, lambda block: block, finish1)
-
-    send_halo(1, lambda one_hot: dot(one_hot, hidden[...]), outgoing2, halo2)
+    own1(0)
+    own1(1)
+
+    for h in range(2):
+        half = pl.ds(h * 256, 256)
+        for g in range(4):
+            block, cols, _ = arrived(0, h, g)
+            add = acc[:, half] + dot(adj[:, cols], block)
+            if g < 3:
+                acc[:, half] = add
+            else:
+                hidden[:, half] = jnp.maximum(add, 0.0).astype(BF)
+        send_rows(1, h, lambda one_hot: dot(one_hot, hidden[:, half]))
 
     @pl.loop(0, 4)
     def _(m):
         at = pl.ds(pl.multiple_of(m * 256, 256), 256)
         neigh[at, :] = dot(hidden[at, :], w2v[:, 512:]).astype(BF)
 
-    @pl.loop(0, 4)
+    @pl.loop(0, 2)
     def _(m):
-        at = pl.ds(pl.multiple_of(m * 256, 256), 256)
+        at = pl.ds(pl.multiple_of(m * 512, 512), 512)
         acc[at, :] = dot(hidden[at, :], w2v[:, :512]) + bias2[...] + dot(adj[at, :ND], neigh[...])
 
-    def finish2(m, at, add):
-        result[at, :] = add.astype(BF)
-        pltpu.make_async_copy(result.at[at], out.at[at], o_sem.at[m]).start()
-
-    receive_halo(1, halo2, lambda block: dot(block, w2v[:, 512:]).astype(BF), finish2)
-    for m in range(2):
-        at = pl.ds(m * 512, 512)
-        pltpu.make_async_copy(result.at[at], out.at[at], o_sem.at[m]).wait()
+    for g in range(4):
+        block, _, at = arrived(1, 0, g)
+        part2[at, :] = dot(block, w2v[:256, 512:])
+    for g in range(4):
+        block, cols, at = arrived(1, 1, g)
+        source = (part2[at, :] + dot(block, w2v[256:, 512:])).astype(BF)
+        for m in range(2):
+            at = pl.ds(m * 512, 512)
+            add = acc[at, :] + dot(adj[at, cols], source)
+            if g < 3:
+                acc[at, :] = add
+            else:
+                out[at, :] = add.astype(BF)
 
     sent = xt.at[pl.ds(0, 15)]
     remote(sent, sent, x_send, x_recv.at[0], (dp, mp)).wait_send()
     for phase in range(3):
         for h in range(2):
             w1_phase(phase, h).wait_send()
-    for layer, outgoing in enumerate((outgoing1, outgoing2)):
-        sent = outgoing.at[pl.ds(0, 127)]
-        remote(sent, sent, h_send.at[layer], h_recv.at[layer, 0], (dp, mp)).wait_send()
+    for layer in range(2):
+        for h in range(2):
+            sent = stage.at[layer, h, pl.ds(0, 127)]
+            remote(sent, sent, h_send.at[layer, h], h_recv.at[layer, h, 0], (dp, mp)).wait_send()
 
 
 def shards(
@@ -231,11 +247,12 @@
     vmem = pl.BlockSpec(memory_space=pltpu.VMEM)
     smem = pl.BlockSpec(memory_space=pltpu.SMEM)
     dma = pltpu.SemaphoreType.DMA
+    keep = lambda a: pltpu.with_memory_space_constraint(a, pltpu.HBM)
     return pl.pallas_call(
         kernel,
         out_shape=jax.ShapeDtypeStruct((ND, HID), BF),
         in_specs=[hbm, hbm, vmem, hbm, vmem, vmem, vmem, vmem, smem, hbm],
-        out_specs=hbm,
+        out_specs=vmem,
         scratch_shapes=[
             pltpu.VMEM((16, 64, ND), BF),
             pltpu.VMEM((16, 64, ND), BF),
@@ -251,21 +268,19 @@
             pltpu.VMEM((HID, ND), BF),
             pltpu.VMEM((ND, HID), BF),
             pltpu.VMEM((ND, HID), BF),
-            pltpu.VMEM((ND, HID), BF),
+            pltpu.VMEM((ND, HID), F32),
             pltpu.VMEM((1, 128), jnp.int32),
             pltpu.SMEM((1, 128), jnp.int32),
-            pltpu.VMEM((128, 8, HID), BF),
-            pltpu.VMEM((128, 8, HID), BF),
-            pltpu.VMEM((128, 8, HID), BF),
-            pltpu.VMEM((128, 8, HID), BF),
-            dma((6, 2)), dma, dma((4,)), dma((3, 2)), dma((3, 2)), dma((2,)), dma((2, 4)), dma((2,)),
+            pltpu.VMEM((2, 2, 128, 8, 256), BF),
+            pltpu.VMEM((2, 2, 128, 8, 256), BF),
+            dma((6, 2)), dma, dma((4,)), dma((3, 2)), dma((3, 2)), dma((2, 2)), dma((2, 2, 4)),
         ],
         compiler_params=pltpu.CompilerParams(
-            collective_id=0, has_side_effects=True, vmem_limit_bytes=56 * 2**20
+            collective_id=0, has_side_effects=True, vmem_limit_bytes=48 * 2**20
         ),
     )(
-        features.T, weights1, bias1.reshape(1, HID), weights2, bias2.reshape(1, HID),
-        send_rows[0].T, tile_dst, tile_src, tile_count, tile_vals[0],
+        keep(features.T), keep(weights1), keep(bias1.reshape(1, HID)), keep(weights2), keep(bias2.reshape(1, HID)),
+        keep(send_rows[0].T), keep(tile_dst), keep(tile_src), tile_count, keep(tile_vals[0]),
     )
 
 

time: 75.8 us -> 70.8 us (0.934)
  Pallas kernels: 72.7 us -> 69 us
  local copies, waits for them, and re-layouts: 2.26 us -> 0.97 us
    pallas_call x1, Pallas kernels: 72.7 us -> 69 us  [shards(): pl.pallas_call(kernel, out_shape=jax.ShapeDtypeStruct((ND, HID), BF), in_...]
    unnamed x1, local copies, waits for them, and re-layouts: 2.26 us -> 0.97 us
where the time goes in v5:
time: 70.8 us; the launch traced here: 70.6 us
  Pallas kernels  69 us (97%)
  local copies, waits for them, and re-layouts  0.97 us (1%)
    pallas_call x1, Pallas kernels, shards(): pl.pallas_call(kernel, out_shape=jax.ShapeDtypeStruct((ND, HID), BF), in_...  69 us

profile of v5, /device:TPU:1, one launch (start us, length us, event | category | flops | bytes accessed | tf_op | source)
XLA Modules:
  0.0 70.6 jit_solution(5432832070566273116)
XLA Ops:
  0.7 69.0 %shard_map.100 = bf16[1024,512]{1,0:T(8,128)(2,1)S(1)} custom-call(bf16[64,16384]{1,0:T(8,128)(2,1)} %bitcast.8, bf16[64,1024]{1,0:T(8,128)(2,1)} %w1.1, f32[1,512]{1,0:T(1,128)} %bitcast.10, bf16[512,1024]{1,0:T(8,128)(2,1)} %w2.1, f32[1,512]{1,0:T(1,128)} %bitcast.11, s32[8,128]{1,0:T(8,128)} %bitcast.9, s32[1,128]{1,0:T(1,128)} %dst.1, ...), custom_call_target="tpu_custom_call" | custom-call | tf_op jit(solution)/shard_map/pallas_call | solution.py:251
  69.7 1.0 %copy.13 = bf16[1024,512]{1,0:T(8,128)(2,1)} copy(bf16[1024,512]{1,0:T(8,128)(2,1)S(1)} %shard_map.100) | data formatting | bytes 2097152

commit v6 on v5

--- a/solution.py
+++ b/solution.py
@@ -9,6 +9,7 @@
 ND, F, HID, TILE = 1024, 1024, 512, 128
 STEPS = (2, 1, 3, 0)
 PLANE = ((2, 2), (2, 1), (1, 2), (2, 3), (3, 2), (0, 2), (2, 0), (1, 1), (3, 3), (1, 3), (3, 1), (0, 1), (1, 0), (0, 3), (3, 0))
+E1, E2 = 9, 12
 BF = jnp.bfloat16
 F32 = jnp.float32
 
@@ -94,8 +95,11 @@
             block = w1f.at[h, c, x, mp]
             remote(block, block, w_send.at[0, h], w_recv.at[0, h], (dp, p)).start()
 
-    for (a, b), p in zip(PLANE, plane):
-        remote(xs.at[p], xt.at[mp], x_send, x_recv.at[STEPS.index(a)], (dp, p)).start()
+    def send_features(first, end):
+        for (a, b), p in list(zip(PLANE, plane))[first:end]:
+            remote(xs.at[p], xt.at[mp], x_send, x_recv.at[STEPS.index(a)], (dp, p)).start()
+
+    send_features(0, E1)
     xt_mine = pltpu.make_async_copy(xs.at[mp], xt.at[mp], local_sem.at[5, 0])
     xt_mine.start()
 
@@ -108,6 +112,8 @@
         for there in along_x:
             part = w1f.at[h, c, x]
             remote(part, part, w_send.at[1, h], w_recv.at[1, h], there).start()
+        if h == 1:
+            send_features(E1, E2)
 
     tiles_in.wait()
     slot_in.wait()
@@ -121,6 +127,8 @@
     for h in (1, 0):
         w1_phase(1, h).wait_recv()
         remote(w1f.at[h, c], w1f.at[h, c], w_send.at[2, h], w_recv.at[2, h], sibling).start()
+        if h == 1:
+            send_features(E2, 15)
 
     def w1_columns(h, k):
         return w1f[h, :, k].swapaxes(0, 1).reshape(F, 128)

time: 70.8 us -> 69.3 us (0.979)
  Pallas kernels: 69 us -> 67.5 us
    pallas_call x1, Pallas kernels: 69 us -> 67.5 us  [shards(): pl.pallas_call(kernel, out_shape=jax.ShapeDtypeStruct((ND, HID), BF), in_...]
where the time goes in v6:
time: 69.3 us; the launch traced here: 69.1 us
  Pallas kernels  67.5 us (97%)
  local copies, waits for them, and re-layouts  0.97 us (1%)
    pallas_call x1, Pallas kernels, shards(): pl.pallas_call(kernel, out_shape=jax.ShapeDtypeStruct((ND, HID), BF), in_...  67.5 us

profile of v6, /device:TPU:1, one launch (start us, length us, event | category | flops | bytes accessed | tf_op | source)
XLA Modules:
  0.0 69.1 jit_solution(3002661242487312444)
XLA Ops:
  0.7 67.5 %shard_map.100 = bf16[1024,512]{1,0:T(8,128)(2,1)S(1)} custom-call(bf16[64,16384]{1,0:T(8,128)(2,1)} %bitcast.8, bf16[64,1024]{1,0:T(8,128)(2,1)} %w1.1, f32[1,512]{1,0:T(1,128)} %bitcast.10, bf16[512,1024]{1,0:T(8,128)(2,1)} %w2.1, f32[1,512]{1,0:T(1,128)} %bitcast.11, s32[8,128]{1,0:T(8,128)} %bitcast.9, s32[1,128]{1,0:T(1,128)} %dst.1, ...), custom_call_target="tpu_custom_call" | custom-call | tf_op jit(solution)/shard_map/pallas_call | solution.py:259
  68.2 1.0 %copy.13 = bf16[1024,512]{1,0:T(8,128)(2,1)} copy(bf16[1024,512]{1,0:T(8,128)(2,1)S(1)} %shard_map.100) | data formatting | bytes 2097152

commit v7 on v6

--- a/solution.py
+++ b/solution.py
@@ -159,15 +159,14 @@
         for g, dx in enumerate(STEPS):
             at = pl.ds(pl.multiple_of(xs_at[dx] * 256, 256), 256)
             stage[layer, h, pl.ds(xs_at[dx] * 32, 32)] = picked(pick[at, :]).reshape(32, 8, 256).astype(BF)
-            for a in STEPS:
-                for b in STEPS:
-                    for e in (1, 0):
-                        if (dx, a, b, e) != (0, 0, 0, 0):
-                            there_dp, there_mp = xs_at[dx] * 2 + cs_at[e], ys_at[a] + zs_at[b]
-                            remote(
-                                stage.at[layer, h, there_dp * 16 + there_mp], halo.at[layer, h, dp * 16 + mp],
-                                h_send.at[layer, h], h_recv.at[layer, h, g], (there_dp, there_mp),
-                            ).start()
+            for e in (1, 0):
+                for a, b in PLANE + ((0, 0),):
+                    if (dx, a, b, e) != (0, 0, 0, 0):
+                        there_dp, there_mp = xs_at[dx] * 2 + cs_at[e], ys_at[a] + zs_at[b]
+                        remote(
+                            stage.at[layer, h, there_dp * 16 + there_mp], halo.at[layer, h, dp * 16 + mp],
+                            h_send.at[layer, h], h_recv.at[layer, h, g], (there_dp, there_mp),
+                        ).start()
         halo[layer, h, dp * 16 + mp] = stage[layer, h, dp * 16 + mp]
 
     def arrived(layer, h, g):

time: 69.3 us -> 68 us (0.981)
  Pallas kernels: 67.5 us -> 66.2 us
    pallas_call x1, Pallas kernels: 67.5 us -> 66.2 us  [shards(): pl.pallas_call(kernel, out_shape=jax.ShapeDtypeStruct((ND, HID), BF), in_...]
where the time goes in v7:
time: 68 us; the launch traced here: 67.9 us
  Pallas kernels  66.2 us (97%)
  local copies, waits for them, and re-layouts  0.97 us (1%)
    pallas_call x1, Pallas kernels, shards(): pl.pallas_call(kernel, out_shape=jax.ShapeDtypeStruct((ND, HID), BF), in_...  66.2 us

profile of v7, /device:TPU:1, one launch (start us, length us, event | category | flops | bytes accessed | tf_op | source)
XLA Modules:
  0.0 67.9 jit_solution(2130367658920963274)
XLA Ops:
  0.7 66.2 %shard_map.100 = bf16[1024,512]{1,0:T(8,128)(2,1)S(1)} custom-call(bf16[64,16384]{1,0:T(8,128)(2,1)} %bitcast.8, bf16[64,1024]{1,0:T(8,128)(2,1)} %w1.1, f32[1,512]{1,0:T(1,128)} %bitcast.10, bf16[512,1024]{1,0:T(8,128)(2,1)} %w2.1, f32[1,512]{1,0:T(1,128)} %bitcast.11, s32[8,128]{1,0:T(8,128)} %bitcast.9, s32[1,128]{1,0:T(1,128)} %dst.1, ...), custom_call_target="tpu_custom_call" | custom-call | tf_op jit(solution)/shard_map/pallas_call | solution.py:258
  66.9 1.0 %copy.13 = bf16[1024,512]{1,0:T(8,128)(2,1)} copy(bf16[1024,512]{1,0:T(8,128)(2,1)S(1)} %shard_map.100) | data formatting | bytes 2097152
